TPU v7x, 32 devices: a whole 2x2x4 slice. The times are simulated.
32 devices in a mesh: chan: 8 (over z, x), tm: 4 (over y, core).
Axes of the slice: x: 2, y: 2, z: 4, core: 2. Of those that a mesh axis runs over, the one named last changes fastest.
Arguments:
- voltages: bfloat16 [2, 2, 8, 2048, 2048], P(None, None, None, 'chan', 'tm'), may hold values from -6 to 6
- weights: bfloat16 [8, 2, 2, 32, 2048], P('chan'), may hold values from -0.09375 to 0.09375
- channel_map: int32 [8], replicated, may hold values from 0 to 7, each once
- sweep_response_taps: float32 [8, 2, 32, 256], P('chan', None, 'tm'), may hold values from -6 to 6
- chirp_length: int32 [32], P('tm'), may hold values from 32 to 256, as said below
Outputs:
- dedispersed: float32 [8, 2, 2, 32, 2048], P('chan', None, None, 'tm')
Inputs may be any that keep to these rules, and one draw needn't show every extreme that they name: `channel_map`: each channel appears once. `chirp_length`: one beam has the longest chirp of exactly 256 samples.
All inputs are finite; a program needn't handle non-finite values.
Results may differ from a plain program's by a relative error of at most 0.0003.
Values may be sent and summed in bfloat16 or wider, within the bound.
A program may use at most 128 MiB of HBM per device.

v0:
```python
import math

import jax
import jax.numpy as jnp
from jax import lax
from jax.sharding import PartitionSpec as P


def mixing_matrix(weight_rows, axis):
    real_part = lax.index_in_dim(weight_rows, 0, axis, keepdims=False)
    imag_part = lax.index_in_dim(weight_rows, 1, axis, keepdims=False)
    upper = jnp.stack([real_part, -imag_part], axis=-2)
    lower = jnp.stack([imag_part, real_part], axis=-2)
    return jnp.stack([upper, lower], axis=axis)


def fourier_tables(extent):
    counter = jnp.arange(extent, dtype=jnp.int32)
    phase = counter[:, None] * counter[None, :] % extent
    angle = phase.astype(jnp.float32) * (2.0 * math.pi / extent)
    return (jnp.cos(angle), jnp.sin(angle))


def product(left, right):
    return jnp.matmul(left, right, precision=lax.Precision.HIGHEST)


def build_dedispersion(sweep_response_taps, chirp_length):
    longest = sweep_response_taps.shape[3]
    block_size = 2 * longest
    cosines, sines = fourier_tables(block_size)
    lag = jnp.arange(longest, dtype=jnp.int32)
    inside = lag[None, :] < chirp_length[:, None]
    factor = lax.rsqrt(chirp_length.astype(jnp.float32))[:, None]
    resp_real = jnp.where(inside, sweep_response_taps[0, 0], 0.0) * factor
    resp_imag = jnp.where(inside, sweep_response_taps[0, 1], 0.0) * factor
    freq_real = product(resp_real, cosines[:longest]) + product(resp_imag, sines[:longest])
    freq_imag = product(resp_imag, cosines[:longest]) - product(resp_real, sines[:longest])
    gain_real = freq_real[:, None, :]
    gain_imag = freq_imag[:, None, :]
    back_cos = cosines[:, longest:]
    back_sin = sines[:, longest:]

    def dedisperse(series):
        total = series.shape[3]
        count = total // longest
        padding = jnp.zeros(series.shape[:3] + (longest,), jnp.float32)
        padded = jnp.concatenate([padding, series], axis=3)
        front = padded[..., :total].reshape(series.shape[:3] + (count, longest))
        behind = padded[..., longest:].reshape(series.shape[:3] + (count, longest))
        blocks = jnp.concatenate([front, behind], axis=4)
        spec_real = product(blocks[0], cosines) + product(blocks[1], sines)
        spec_imag = product(blocks[1], cosines) - product(blocks[0], sines)
        prod_real = spec_real * gain_real - spec_imag * gain_imag
        prod_imag = spec_real * gain_imag + spec_imag * gain_real
        out_real = (product(prod_real, back_cos) - product(prod_imag, back_sin)) / block_size
        out_imag = (product(prod_imag, back_cos) + product(prod_real, back_sin)) / block_size
        return jnp.stack([out_real, out_imag], 0).reshape(series.shape)

    return dedisperse


def on_device(voltages, weights, channel_map, sweep_response_taps, chirp_length):
    selected = jnp.take(voltages, channel_map, axis=2)
    mixing = mixing_matrix(weights[0], 0)
    beams = jnp.einsum(
        "opbra,rpat->opbt",
        mixing,
        lax.all_to_all(selected, "chan", split_axis=2, concat_axis=3, tiled=True)[:, :, 0],
        preferred_element_type=jnp.float32,
    )
    dedisperse = build_dedispersion(sweep_response_taps, chirp_length)
    result = dedisperse(lax.all_to_all(beams, "tm", split_axis=2, concat_axis=3, tiled=True))
    return result[None]


def solution(mesh):
    return jax.shard_map(
        on_device,
        mesh=mesh,
        in_specs=(
            P(None, None, None, "chan", "tm"),
            P("chan", None, None, None, None),
            P(),
            P("chan", None, "tm", None),
            P("tm"),
        ),
        out_specs=P("chan", None, None, "tm", None),
        check_vma=False,
    )
```

profile of v0, /device:TPU:5, one launch (start us, length us, event | category | flops | bytes accessed | tf_op | source)
XLA Modules:
  0.0 250.3 jit_solution(4417517409902186092)
XLA Ops:
  0.0 0.7 compare_select_fusion
  0.7 0.7 compare_and_fusion
  1.3 8.1 %gather_fusion = bf16[8,2,2,256,512]{4,3,2,1,0:T(8,128)(2,1)} fusion(bf16[2,2,8,256,512]{4,3,2,1,0:T(8,128)(2,1)} %param.5, s32[1024]{0:T(1024)S(1)} %pad_clamp_fusion), kind=kCustom, calls=%fused_computation | custom fusion | bytes 16777248 | tf_op jit(solution)/shard_map/jit(_take)/gather | solution.py:64
  9.4 7.5 %select_bitcast_fusion = bf16[2,2,8,256,512]{4,3,1,0,2:T(8,128)(2,1)} fusion(bf16[8,2,2,256,512]{4,3,2,1,0:T(8,128)(2,1)} %gather_fusion, pred[8]{0:T(512)(128)(4,1)S(1)} %compare_and_fusion), kind=kLoop, calls=%fused_computation.1 | loop fusion | flops 4194304 | bytes 16777224 | tf_op jit(solution)/shard_map/jit(_take)/select_n | solution.py:64
  16.9 5.7 %all-to-all-start = ((bf16[2,2,8,256,512]{4,3,1,0,2:T(8,128)(2,1)}), bf16[2,2,8,256,512]{4,3,1,0,2:T(8,128)(2,1)}, u32[]{:S(2)}, u32[]{:S(2)}) async-start(bf16[2,2,8,256,512]{4,3,1,0,2:T(8,128)(2,1)} %select_bitcast_fusion), calls=%async_computation | async-start | bytes 16777216 | tf_op jit(solution)/shard_map/all_to_all | solution.py:69
  22.5 3.8 %fusion.18 = f32[512,512]{1,0:T(8,128)S(1)} fusion(), kind=kLoop, calls=%fused_computation.34 | loop fusion | flops 3670016 | bytes 1048576 | tf_op jit(solution)/shard_map/cos | solution.py:21
  26.3 3.8 %fusion.17 = f32[512,512]{1,0:T(8,128)S(1)} fusion(), kind=kLoop, calls=%fused_computation.33 | loop fusion | flops 3670016 | bytes 1048576 | tf_op jit(solution)/shard_map/sin | solution.py:21
  30.6 0.4 fusion.25
  30.9 0.4 convolution_add_fusion.2
  31.5 173.4 %all-to-all-done = bf16[2,2,8,256,512]{4,3,1,0,2:T(8,128)(2,1)} async-done(((bf16[2,2,8,256,512]{4,3,1,0,2:T(8,128)(2,1)}), bf16[2,2,8,256,512]{4,3,1,0,2:T(8,128)(2,1)}, u32[]{:S(2)}, u32[]{:S(2)}) %all-to-all-start) | async-done | bytes 8388640 | tf_op jit(solution)/shard_map/all_to_all | solution.py:69
  204.8 7.5 %copy.12 = bf16[2,2,8,256,512]{4,3,2,0,1:T(8,128)(2,1)} copy(bf16[2,2,8,256,512]{4,3,1,0,2:T(8,128)(2,1)} %all-to-all-done) | data formatting | bytes 16777216 | tf_op jit(solution)/shard_map/all_to_all | solution.py:69
  212.3 4.9 %convolution_bitcast_fusion = f32[2,2,32,512]{3,2,0,1:T(8,128)S(1)} fusion(bf16[2,2,2048,512,1]{3,2,0,4,1:T(8,128)(2,1)} %bitcast.84, bf16[1,2,32,2,2048]{4,2,3,0,1:T(8,128)(2,1)S(1)} %get-tuple-element.8, bf16[1,2,32,2,2048]{4,2,3,0,1:T(8,128)(2,1)S(1)} %get-tuple-element.7), kind=kOutput, calls=%fused_computation.7 | convolution fusion | flops 538968064 | bytes 9699328 | tf_op jit(solution)/shard_map/opbra,rpat->opbt/dot_general | solution.py:66
  217.3 0.9 copy.14
  218.2 5.3 %all-to-all-start.1 = ((f32[2,2,32,512]{3,0,1,2:T(2,128)}), f32[2,2,32,512]{3,0,1,2:T(2,128)S(1)}, u32[]{:S(2)}, u32[]{:S(2)}) async-start(f32[2,2,32,512]{3,0,1,2:T(2,128)} %copy.14), calls=%async_computation.1 | async-start | bytes 524288 | tf_op jit(solution)/shard_map/all_to_all | solution.py:73
  223.9 3.7 %all-to-all-done.1 = f32[2,2,32,512]{3,0,1,2:T(2,128)S(1)} async-done(((f32[2,2,32,512]{3,0,1,2:T(2,128)}), f32[2,2,32,512]{3,0,1,2:T(2,128)S(1)}, u32[]{:S(2)}, u32[]{:S(2)}) %all-to-all-start.1) | async-done | bytes 262176 | tf_op jit(solution)/shard_map/all_to_all | solution.py:73
  228.2 4.9 %fusion.12 = f32[2,8,8,512]{3,2,1,0:T(8,128)S(1)} fusion(f32[2,2,8,8,512]{4,3,2,1,0:T(8,128)S(1)} %constant_dynamic-update-slice_fusion), kind=kOutput, calls=%fused_computation.24 | convolution fusion | flops 406323200 | bytes 524288 | tf_op jit(solution)/shard_map/dot_general | solution.py:25
  233.1 4.9 %fusion.10 = f32[2,8,8,512]{3,2,1,0:T(8,128)S(1)} fusion(f32[2,2,8,8,512]{4,3,2,1,0:T(8,128)S(1)} %constant_dynamic-update-slice_fusion), kind=kOutput, calls=%fused_computation.22 | convolution fusion | flops 406323200 | bytes 524288 | tf_op jit(solution)/shard_map/dot_general | solution.py:25
  238.0 4.9 %convolution_add_fusion = f32[2,8,8,512]{3,2,1,0:T(8,128)S(1)} fusion(f32[2,8,8,512]{3,2,1,0:T(8,128)S(1)} %fusion.12, f32[2,2,8,8,512]{4,3,2,1,0:T(8,128)S(1)} %constant_dynamic-update-slice_fusion), kind=kOutput, calls=%fused_computation.6 | convolution fusion | flops 406388736 | bytes 786432 | tf_op jit(solution)/shard_map/dot_general | solution.py:25
  242.9 4.9 %convolution_subtract_fusion = f32[2,8,8,512]{3,2,1,0:T(8,128)S(1)} fusion(f32[2,8,8,512]{3,2,1,0:T(8,128)S(1)} %fusion.10, f32[2,2,8,8,512]{4,3,2,1,0:T(8,128)S(1)} %constant_dynamic-update-slice_fusion), kind=kOutput, calls=%fused_computation.5 | convolution fusion | flops 406388736 | bytes 786432 | tf_op jit(solution)/shard_map/dot_general | solution.py:25
  247.7 0.4 fusion.30
  248.2 0.4 fusion.29
  248.6 0.4 fusion.1
  249.1 0.4 fusion
  249.6 0.7 pad_maximum_fusion
  (22 shorter events, 1.6 us)
Async XLA Ops:
  16.9 13.3 %copy-start.2 = (s32[8]{0:T(128)S(1)}, s32[8]{0:T(128)}, u32[]{:S(2)}) copy-start(s32[8]{0:T(128)} %param.9) | copy-start | bytes 100
  16.9 13.3 %copy-start.1 = (f32[1,2,8,256]{3,2,1,0:T(8,128)S(1)}, f32[1,2,8,256]{3,2,1,0:T(8,128)}, u32[]{:S(2)}) copy-start(f32[1,2,8,256]{3,2,1,0:T(8,128)} %param.8) | copy-start | bytes 49156
  16.9 14.4 %copy-start = (bf16[1,2,2,32,2048]{4,3,2,1,0:T(8,128)(2,1)S(1)}, bf16[1,2,2,32,2048]{4,3,2,1,0:T(8,128)(2,1)}, u32[]{:S(2)}) copy-start(bf16[1,2,2,32,2048]{4,3,2,1,0:T(8,128)(2,1)} %param.6) | copy-start | bytes 1572868
  16.9 188.0 %all-to-all-start = ((bf16[2,2,8,256,512]{4,3,1,0,2:T(8,128)(2,1)}), bf16[2,2,8,256,512]{4,3,1,0,2:T(8,128)(2,1)}, u32[]{:S(2)}, u32[]{:S(2)}) async-start(bf16[2,2,8,256,512]{4,3,1,0,2:T(8,128)(2,1)} %select_bitcast_fusion), calls=%async_computation | async-start | bytes 16777216 | tf_op jit(solution)/shard_map/all_to_all | solution.py:69
  218.2 9.4 %all-to-all-start.1 = ((f32[2,2,32,512]{3,0,1,2:T(2,128)}), f32[2,2,32,512]{3,0,1,2:T(2,128)S(1)}, u32[]{:S(2)}, u32[]{:S(2)}) async-start(f32[2,2,32,512]{3,0,1,2:T(2,128)} %copy.14), calls=%async_computation.1 | async-start | bytes 524288 | tf_op jit(solution)/shard_map/all_to_all | solution.py:73
where the time goes:
time: 253 us; the launch traced here: 250 us
  waiting for transfers between devices  177 us (70%)
  matrix products  27.6 us (11%)
  other arithmetic  17.2 us (7%)
  local copies, waits for them, and re-layouts  17.2 us (7%)
  starting transfers between devices  11 us (4%)
    all_to_all x1, waiting for transfers between devices, on_device(): lax.all_to_all(selected, 'chan', split_axis=2, concat_axis=3, tiled=True)  173 us
    dot_general x12, matrix products, product(): return jnp.matmul(left, right, precision=lax.Precision.HIGHEST)  22.7 us
    select_n x2, other arithmetic, on_device(): selected = jnp.take(voltages, channel_map, axis=2)  8.14 us
    gather x1, local copies, waits for them, and re-layouts, on_device(): selected = jnp.take(voltages, channel_map, axis=2)  8.07 us
    all_to_all x1, local copies, waits for them, and re-layouts, on_device(): lax.all_to_all(selected, 'chan', split_axis=2, concat_axis=3, tiled=True)  7.49 us
    all_to_all x1, starting transfers between devices, on_device(): lax.all_to_all(selected, 'chan', split_axis=2, concat_axis=3, tiled=True)  5.66 us
    all_to_all x1, starting transfers between devices, on_device(): lax.all_to_all(beams, 'tm', split_axis=2, concat_axis=3, tiled=True)  5.34 us
  transfers between devices with their start and end apart: 2, of which 2 were waited for; matrix products, arithmetic and copies ran while one was open for 4% of the time, Pallas kernels for 0%

commit v1 on v0

v1 whole, which is shorter than its diff:
```python
import functools
import math

import jax
import jax.numpy as jnp
import ml_dtypes
import numpy as np
from jax import lax
from jax.experimental import pallas as pl
from jax.experimental.pallas import tpu as pltpu
from jax.sharding import PartitionSpec as P

TOP = 32767.0
MESH = pl.DeviceIdType.MESH


def dot(left, right):
    return jnp.dot(left, right, preferred_element_type=jnp.float32)


def fourier_tables(extent):
    counter = np.arange(extent, dtype=np.int64)
    angle = (counter[:, None] * counter[None, :] % extent) * (2.0 * math.pi / extent)
    tables = []
    for table in (np.cos(angle), np.sin(angle)):
        high = table.astype(ml_dtypes.bfloat16)
        low = (table - high.astype(np.float64)).astype(ml_dtypes.bfloat16)
        tables += [high, low]
    return np.stack(tables)


def beam_kernel(groups, map_ref, volt_ref, weight_ref, code_ref, step_ref):
    pols, beams = weight_ref.shape[2], weight_ref.shape[3]
    reals, imags = [], []
    for p in range(pols):
        mixed = jnp.concatenate([weight_ref[0, 0, p], weight_ref[0, 1, p]], axis=0)
        left = dot(mixed, volt_ref[0, p, 0])
        right = dot(mixed, volt_ref[1, p, 0])
        reals.append(left[:beams] - right[beams:])
        imags.append(left[beams:] + right[:beams])
    share = beams // groups
    for g in range(groups):
        rows = jnp.concatenate([part[g * share : (g + 1) * share] for part in reals + imags], axis=0)
        peak = jnp.maximum(jnp.max(jnp.abs(rows), axis=0, keepdims=True), 1e-30)
        codes = jnp.round(rows * (TOP / peak)).astype(jnp.int32)
        code_ref[0, g] = codes.astype(jnp.int16)
        step_ref[0, g] = peak * (1.0 / TOP)


def form_beams(voltages, weights, channel_map, groups):
    parts, pols, channels, antennas, times = voltages.shape
    slots, beams = weights.shape[0], weights.shape[3]
    rows = 2 * pols * beams // groups
    return pl.pallas_call(
        functools.partial(beam_kernel, groups),
        grid_spec=pltpu.PrefetchScalarGridSpec(
            num_scalar_prefetch=1,
            grid=(slots,),
            in_specs=[
                pl.BlockSpec((parts, pols, 1, antennas, times), lambda j, m: (0, 0, m[j], 0, 0)),
                pl.BlockSpec((1, 2, pols, beams, antennas), lambda j, m: (j, 0, 0, 0, 0)),
            ],
            out_specs=[
                pl.BlockSpec((1, groups, rows, times), lambda j, m: (j, 0, 0, 0)),
                pl.BlockSpec((1, groups, 1, times), lambda j, m: (j, 0, 0, 0)),
            ],
        ),
        out_shape=[
            jax.ShapeDtypeStruct((slots, groups, rows, times), jnp.int16),
            jax.ShapeDtypeStruct((slots, groups, 1, times), jnp.float32),
        ],
        compiler_params=pltpu.CompilerParams(vmem_limit_bytes=24 << 20),
        name="form_beams",
    )(channel_map, voltages, weights)


def exchange_kernel(chans, groups, code_ref, step_ref, code_out, step_out, send, recv, own):
    chan, group = lax.axis_index("chan"), lax.axis_index("tm")
    total = chans * groups
    me = chan * groups + group
    barrier = pltpu.get_barrier_semaphore()

    def place(k):
        other = lax.rem(me + k, total)
        return other, (lax.div(other, groups), lax.rem(other, groups))

    @pl.loop(1, total)
    def _(k):
        pl.semaphore_signal(barrier, inc=1, device_id=place(k)[1], device_id_type=MESH)

    mine = [
        pltpu.make_async_copy(code_ref.at[me], code_out.at[me], own.at[0]),
        pltpu.make_async_copy(step_ref.at[me], step_out.at[me], own.at[1]),
    ]
    for copy in mine:
        copy.start()
    pl.semaphore_wait(barrier, total - 1)

    def copies(source, target, slot, device):
        return [
            pltpu.make_async_remote_copy(
                src_ref=a.at[source], dst_ref=b.at[target], send_sem=send.at[n, slot],
                recv_sem=recv.at[n, target], device_id=device, device_id_type=MESH,
            )
            for n, (a, b) in enumerate(((code_ref, code_out), (step_ref, step_out)))
        ]

    @pl.loop(1, total)
    def _(k):
        other, device = place(k)
        for copy in copies(other, me, k, device):
            copy.start()

    @pl.loop(1, total)
    def _(k):
        other, device = place(k)
        for copy in copies(other, other, k, device):
            copy.wait_send()
            copy.wait_recv()

    for copy in mine:
        copy.wait()


def exchange(codes, steps, chans, groups):
    total = chans * groups
    return pl.pallas_call(
        functools.partial(exchange_kernel, chans, groups),
        in_specs=[pl.BlockSpec(memory_space=pl.ANY)] * 2,
        out_specs=[pl.BlockSpec(memory_space=pl.ANY)] * 2,
        out_shape=[jax.ShapeDtypeStruct(a.shape, a.dtype) for a in (codes, steps)],
        scratch_shapes=[
            pltpu.SemaphoreType.DMA((2, total)),
            pltpu.SemaphoreType.DMA((2, total)),
            pltpu.SemaphoreType.DMA((2,)),
        ],
        compiler_params=pltpu.CompilerParams(collective_id=0, has_side_effects=True),
        name="exchange",
    )(codes, steps)


def split(value):
    high = value.astype(jnp.bfloat16)
    return high, (value - high.astype(jnp.float32)).astype(jnp.bfloat16)


def transform(value, high, low):
    rows = value.shape[0]
    first, second = split(value)
    both = dot(jnp.concatenate([first, second], axis=0), high)
    return both[:rows] + both[rows:] + dot(first, low)


def dedisperse_kernel(chans, groups, code_ref, step_ref, resp_ref, table_ref, out_ref, sums):
    longest, beams = resp_ref.shape[2], resp_ref.shape[1]
    rows, times = code_ref.shape[1], code_ref.shape[2]
    half = rows // 2
    for g in range(groups):

        def add(c, total, g=g):
            at = c * groups + g
            return total + code_ref[at].astype(jnp.int32).astype(jnp.float32) * step_ref[at]

        sums[g] = lax.fori_loop(0, chans, add, jnp.zeros((rows, times), jnp.float32))
    cos_high, cos_low, sin_high, sin_low = (table_ref[n] for n in range(4))
    resp = jnp.concatenate([resp_ref[0], resp_ref[1]], axis=0)
    by_cos = transform(resp, cos_high[:longest], cos_low[:longest])
    by_sin = transform(resp, sin_high[:longest], sin_low[:longest])
    gain_real = (by_cos[:beams] + by_sin[beams:])[None]
    gain_imag = (by_cos[beams:] - by_sin[:beams])[None]

    per = times // longest
    count = groups * per
    blocks = []
    for r in range(2):
        pieces = [jnp.zeros((half, longest), jnp.float32)]
        for m in range(count):
            pieces.append(sums[m // per, r * half : (r + 1) * half, (m % per) * longest : (m % per + 1) * longest])
        blocks += [jnp.concatenate([pieces[m], pieces[m + 1]], axis=1) for m in range(count)]
    stacked = jnp.concatenate(blocks, axis=0)
    size = count * half
    by_cos = transform(stacked, cos_high, cos_low)
    by_sin = transform(stacked, sin_high, sin_low)
    shape = (size // beams, beams, 2 * longest)
    spec_real = (by_cos[:size] + by_sin[size:]).reshape(shape)
    spec_imag = (by_cos[size:] - by_sin[:size]).reshape(shape)
    prod_real = (spec_real * gain_real - spec_imag * gain_imag).reshape(size, 2 * longest)
    prod_imag = (spec_real * gain_imag + spec_imag * gain_real).reshape(size, 2 * longest)
    stacked = jnp.concatenate([prod_real, prod_imag], axis=0) * (0.5 / longest)
    by_cos = transform(stacked, cos_high[:, longest:], cos_low[:, longest:])
    by_sin = transform(stacked, sin_high[:, longest:], sin_low[:, longest:])
    results = (by_cos[:size] - by_sin[size:], by_cos[size:] + by_sin[:size])
    for r in range(2):
        for m in range(count):
            for p in range(half // beams):
                start = m * half + p * beams
                out_ref[0, r, p, :, m * longest : (m + 1) * longest] = results[r][start : start + beams]


def dedisperse(codes, steps, resp, chans, groups):
    rows, times = codes.shape[1:]
    beams, longest = resp.shape[1:]
    return pl.pallas_call(
        functools.partial(dedisperse_kernel, chans, groups),
        in_specs=[pl.BlockSpec(memory_space=pltpu.VMEM)] * 4,
        out_specs=pl.BlockSpec(memory_space=pltpu.VMEM),
        out_shape=jax.ShapeDtypeStruct((1, 2, rows // (2 * beams), beams, groups * times), jnp.float32),
        scratch_shapes=[pltpu.VMEM((groups, rows, times), jnp.float32)],
        compiler_params=pltpu.CompilerParams(vmem_limit_bytes=40 << 20),
        name="dedisperse",
    )(codes, steps, resp, jnp.asarray(fourier_tables(2 * longest)))


def on_device(chans, groups, voltages, weights, channel_map, sweep_response_taps, chirp_length):
    parts, pols, beams, antennas = weights.shape[1:]
    longest = sweep_response_taps.shape[3]
    pieces = weights[0].reshape(parts, pols, beams, chans, antennas // chans).transpose(3, 0, 1, 2, 4)
    pieces = lax.all_to_all(pieces, "chan", split_axis=0, concat_axis=0, tiled=True)
    lag = jnp.arange(longest, dtype=jnp.int32)
    inside = lag[None, :] < chirp_length[:, None]
    factor = lax.rsqrt(chirp_length.astype(jnp.float32))[:, None]
    resp = jnp.where(inside, sweep_response_taps[0], 0.0) * factor
    codes, steps = form_beams(voltages, pieces, channel_map, groups)
    total = chans * groups
    codes, steps = exchange(codes.reshape((total,) + codes.shape[2:]), steps.reshape((total,) + steps.shape[2:]), chans, groups)
    return dedisperse(codes, steps, resp, chans, groups)


def solution(mesh):
    return jax.shard_map(
        functools.partial(on_device, mesh.shape["chan"], mesh.shape["tm"]),
        mesh=mesh,
        in_specs=(
            P(None, None, None, "chan", "tm"),
            P("chan", None, None, None, None),
            P(),
            P("chan", None, "tm", None),
            P("tm"),
        ),
        out_specs=P("chan", None, None, "tm", None),
        check_vma=False,
    )
```

time: 253 us -> 69.7 us (0.28)
  the two profiles are of different devices: /device:TPU:5 before, /device:TPU:11 now
where the time goes in v1:
time: 69.7 us; the launch traced here: 69.3 us
  Pallas kernels  41.7 us (60%)
  local copies, waits for them, and re-layouts  9.9 us (14%)
  waiting for transfers between devices  9.78 us (14%)
  starting transfers between devices  5.66 us (8%)
  other arithmetic  2.18 us (3%)
    pallas_call x1, Pallas kernels, exchange(): pl.pallas_call(functools.partial(exchange_kernel, chans, groups), in_spec...  34.3 us
    all_to_all x1, waiting for transfers between devices, on_device(): lax.all_to_all(pieces, 'chan', split_axis=0, concat_axis=0, tiled=True)  9.78 us
    unnamed x15, local copies, waits for them, and re-layouts  8.99 us
    all_to_all x1, starting transfers between devices, on_device(): lax.all_to_all(pieces, 'chan', split_axis=0, concat_axis=0, tiled=True)  5.66 us
    pallas_call x1, Pallas kernels, form_beams(): pl.pallas_call(functools.partial(beam_kernel, groups), grid_spec=pltpu.Pr...  4.03 us
    pallas_call x1, Pallas kernels, dedisperse(): pl.pallas_call(functools.partial(dedisperse_kernel, chans, groups), in_sp...  3.4 us
  transfers between devices with their start and end apart: 1, of which 1 were waited for; matrix products, arithmetic and copies ran while one was open for 3% of the time, Pallas kernels for 0%

profile of v1, /device:TPU:11, one launch (start us, length us, event | category | flops | bytes accessed | tf_op | source)
XLA Modules:
  0.0 69.3 jit_solution(4400795168514702718)
XLA Ops:
  0.0 0.0 copy-start.1
  0.0 1.3 %copy.8 = bf16[16,8,8,256]{3,2,1,0:T(8,128)(2,1)S(1)} copy(bf16[16,8,8,256]{3,1,2,0:T(8,128)(2,1)} %bitcast.17) | data formatting | bytes 1048576
  1.3 0.9 %copy.10 = bf16[2,2,32,8,256]{4,2,1,0,3:T(8,128)(2,1)} copy(bf16[2,2,32,8,256]{4,3,2,1,0:T(8,128)(2,1)S(1)} %bitcast.16) | data formatting | bytes 1048576 | tf_op jit(solution)/shard_map/reshape;squeeze | solution.py:217
  2.2 5.7 %all-to-all-start = ((bf16[8,2,2,32,256]{4,3,2,1,0:T(8,128)(2,1)}), bf16[8,2,2,32,256]{4,3,2,1,0:T(8,128)(2,1)S(1)}, u32[]{:S(2)}, u32[]{:S(2)}) async-start(bf16[8,2,2,32,256]{4,3,2,1,0:T(8,128)(2,1)} %bitcast.13), calls=%async_computation | async-start | bytes 1048576 | tf_op jit(solution)/shard_map/all_to_all | solution.py:218
  7.9 0.7 convert_rsqrt_fusion
  8.5 0.7 %iota_compare_fusion = pred[8,256]{1,0:T(8,128)(4,1)S(1)} fusion(s32[8]{0:T(128)} %param.10), kind=kLoop, calls=%fused_computation.3 | loop fusion | flops 2048 | bytes 2080 | tf_op jit(solution)/shard_map/lt | solution.py:220
  9.3 0.8 %fusion.resp_ref = f32[2,8,256]{2,1,0:T(8,128)S(1)} fusion(f32[1,2,8,256]{3,2,1,0:T(8,128)} %param.9, f32[8]{0:T(128)S(1)} %convert_rsqrt_fusion, pred[8,256]{1,0:T(8,128)(4,1)S(1)} %iota_compare_fusion), kind=kLoop, calls=%fused_computation.2 | loop fusion | flops 8192 | bytes 34848 | tf_op jit(solution)/shard_map/mul | solution.py:222
  10.1 9.8 %all-to-all-done.weight_ref = bf16[8,2,2,32,256]{4,3,2,1,0:T(8,128)(2,1)S(1)} async-done(((bf16[8,2,2,32,256]{4,3,2,1,0:T(8,128)(2,1)}), bf16[8,2,2,32,256]{4,3,2,1,0:T(8,128)(2,1)S(1)}, u32[]{:S(2)}, u32[]{:S(2)}) %all-to-all-start) | async-done | bytes 524320 | tf_op jit(solution)/shard_map/all_to_all | solution.py:218
  19.8 0.0 copy-start
  19.8 3.4 %copy-done = bf16[2,2,8,256,512]{4,3,2,1,0:T(8,128)(2,1)S(1)} copy-done((bf16[2,2,8,256,512]{4,3,2,1,0:T(8,128)(2,1)S(1)}, bf16[2,2,8,256,512]{4,3,2,1,0:T(8,128)(2,1)}, u32[]{:S(2)}) %copy-start) | copy-done | bytes 8388632
  23.2 0.0 copy-start.6
  23.2 0.7 copy-done.6
  23.9 4.0 %form_beams.1 = (s16[8,4,32,512]{3,2,1,0:T(8,128)(2,1)S(1)}, f32[8,4,1,512]{3,2,1,0:T(1,128)S(1)}) custom-call(s32[8]{0:T(128)S(1)} %copy-done.6, bf16[2,2,8,256,512]{4,3,2,1,0:T(8,128)(2,1)S(1)} %copy-done, bf16[8,2,2,32,256]{4,3,2,1,0:T(8,128)(2,1)S(1)} %all-to-all-done.weight_ref), custom_call_target="tpu_custom_call" | custom-call | tf_op jit(solution)/shard_map/form_beams/pallas_call | solution.py:54
  27.9 0.0 copy-start.3
  27.9 1.0 %copy-done.3 = s16[8,4,32,512]{3,2,1,0:T(8,128)(2,1)} copy-done((s16[8,4,32,512]{3,2,1,0:T(8,128)(2,1)}, s16[8,4,32,512]{3,2,1,0:T(8,128)(2,1)S(1)}, u32[]{:S(2)}) %copy-start.3) | copy-done | bytes 1048600
  28.9 0.0 copy-start.5
  28.9 0.6 copy-done.5
  29.5 34.3 %exchange.1 = (s16[32,32,512]{2,1,0:T(8,128)(2,1)}, f32[32,1,512]{2,1,0:T(1,128)}) custom-call(s16[32,32,512]{2,1,0:T(8,128)(2,1)} %bitcast.14, f32[32,1,512]{2,1,0:T(1,128)} %bitcast.15), custom_call_target="tpu_custom_call" | custom-call | tf_op jit(solution)/shard_map/exchange/pallas_call | solution.py:127
  63.8 0.0 copy-done.1
  63.8 0.0 copy-start.2
  63.8 1.2 %copy-done.2 = s16[32,32,512]{2,1,0:T(8,128)(2,1)S(1)} copy-done((s16[32,32,512]{2,1,0:T(8,128)(2,1)S(1)}, s16[32,32,512]{2,1,0:T(8,128)(2,1)}, u32[]{:S(2)}) %copy-start.2) | copy-done | bytes 1048600
  65.0 0.0 copy-start.4
  65.0 0.8 %copy-done.4 = f32[32,1,512]{2,1,0:T(1,128)S(1)} copy-done((f32[32,1,512]{2,1,0:T(1,128)S(1)}, f32[32,1,512]{2,1,0:T(1,128)}, u32[]{:S(2)}) %copy-start.4) | copy-done | bytes 65560
  65.9 3.4 %dedisperse.1 = f32[1,2,2,8,2048]{4,3,2,1,0:T(8,128)} custom-call(s16[32,32,512]{2,1,0:T(8,128)(2,1)S(1)} %copy-done.2, f32[32,1,512]{2,1,0:T(1,128)S(1)} %copy-done.4, f32[2,8,256]{2,1,0:T(8,128)S(1)} %fusion.resp_ref, bf16[4,512,512]{2,1,0:T(8,128)(2,1)S(1)} %copy-done.1), custom_call_target="tpu_custom_call" | custom-call | tf_op jit(solution)/shard_map/dedisperse/pallas_call | solution.py:203
Async XLA Ops:
  0.0 63.8 %copy-start.1 = (bf16[4,512,512]{2,1,0:T(8,128)(2,1)S(1)}, bf16[4,512,512]{2,1,0:T(8,128)(2,1)}, u32[]{:S(2)}) copy-start(bf16[4,512,512]{2,1,0:T(8,128)(2,1)} %constant.4.clone.table_ref) | copy-start | bytes 6291460
  2.2 17.6 %all-to-all-start = ((bf16[8,2,2,32,256]{4,3,2,1,0:T(8,128)(2,1)}), bf16[8,2,2,32,256]{4,3,2,1,0:T(8,128)(2,1)S(1)}, u32[]{:S(2)}, u32[]{:S(2)}) async-start(bf16[8,2,2,32,256]{4,3,2,1,0:T(8,128)(2,1)} %bitcast.13), calls=%async_computation | async-start | bytes 1048576 | tf_op jit(solution)/shard_map/all_to_all | solution.py:218
  19.8 3.4 %copy-start = (bf16[2,2,8,256,512]{4,3,2,1,0:T(8,128)(2,1)S(1)}, bf16[2,2,8,256,512]{4,3,2,1,0:T(8,128)(2,1)}, u32[]{:S(2)}) copy-start(bf16[2,2,8,256,512]{4,3,2,1,0:T(8,128)(2,1)} %volt_ref.1) | copy-start | bytes 25165828
  23.2 0.7 copy-start.6
  27.9 1.0 %copy-start.3 = (s16[8,4,32,512]{3,2,1,0:T(8,128)(2,1)}, s16[8,4,32,512]{3,2,1,0:T(8,128)(2,1)S(1)}, u32[]{:S(2)}) copy-start(s16[8,4,32,512]{3,2,1,0:T(8,128)(2,1)S(1)} %get-tuple-element.9) | copy-start | bytes 3145732
  28.9 0.6 copy-start.5
  63.8 1.2 %copy-start.2 = (s16[32,32,512]{2,1,0:T(8,128)(2,1)S(1)}, s16[32,32,512]{2,1,0:T(8,128)(2,1)}, u32[]{:S(2)}) copy-start(s16[32,32,512]{2,1,0:T(8,128)(2,1)} %get-tuple-element.11.code_ref) | copy-start | bytes 3145732
  65.0 0.8 %copy-start.4 = (f32[32,1,512]{2,1,0:T(1,128)S(1)}, f32[32,1,512]{2,1,0:T(1,128)}, u32[]{:S(2)}) copy-start(f32[32,1,512]{2,1,0:T(1,128)} %get-tuple-element.12.step_ref) | copy-start | bytes 196612

commit v2 on v1

v2 whole, which is shorter than its diff:
```python
import functools
import math

import jax
import jax.numpy as jnp
import ml_dtypes
import numpy as np
from jax import lax
from jax.experimental import pallas as pl
from jax.experimental.pallas import tpu as pltpu
from jax.sharding import PartitionSpec as P

TOP = 32767.0
MESH = pl.DeviceIdType.MESH


def dot(left, right):
    return jnp.dot(left, right, preferred_element_type=jnp.float32)


def fourier_tables(extent):
    counter = np.arange(extent, dtype=np.int64)
    angle = (counter[:, None] * counter[None, :] % extent) * (2.0 * math.pi / extent)
    tables = []
    for table in (np.cos(angle), np.sin(angle)):
        high = table.astype(ml_dtypes.bfloat16)
        low = (table - high.astype(np.float64)).astype(ml_dtypes.bfloat16)
        tables += [high, low]
    return np.stack(tables)


def encode(rows):
    peak = jnp.maximum(jnp.max(jnp.abs(rows), axis=0, keepdims=True), 1e-30)
    codes = jnp.round(rows * (TOP / peak)).astype(jnp.int32).astype(jnp.int16)
    return codes, peak * (1.0 / TOP)


def decode(codes, step):
    return codes.astype(jnp.int32).astype(jnp.float32) * step


def form_kernel(
    chans, groups, sliced, map_ref, volt_ref, weight_ref, code_out, step_out,
    volts, mixes, away_code, away_step, near_code, near_step, sum_code, sum_step,
    own, weight_send, weight_recv, pass_send, pass_recv, near_send, near_recv, sum_send, sum_recv,
):
    pols, beams, antennas = mixes.shape[0], mixes.shape[3], mixes.shape[4]
    chan, group = lax.axis_index("chan"), lax.axis_index("tm")
    far, side = lax.div(chan, 2), lax.rem(chan, 2)
    fars = chans // 2
    half = lax.rem(group, 2)
    sibling = (chan, group + 1 - 2 * half)
    partner = (chan + 1 - 2 * side, group)
    total = chans * groups
    me = chan * groups + group
    barrier = pltpu.get_barrier_semaphore()

    @pl.loop(1, total)
    def _(k):
        other = lax.rem(me + k, total)
        device = (lax.div(other, groups), lax.rem(other, groups))
        pl.semaphore_signal(barrier, inc=1, device_id=device, device_id_type=MESH)

    def piece(p, target):
        if sliced:
            return weight_ref.at[:, p, :, pl.ds(pl.multiple_of(target * antennas, antennas), antennas)]
        return weight_ref.at[target, :, p]

    mine = [pltpu.make_async_copy(piece(p, chan), mixes.at[p, chan], own.at[p]) for p in range(pols)]
    load = pltpu.make_async_copy(volt_ref, volts, own.at[pols])
    pl.semaphore_wait(barrier, total - 1)

    def remote(source, target, send, recv, device):
        return pltpu.make_async_remote_copy(
            src_ref=source, dst_ref=target, send_sem=send, recv_sem=recv, device_id=device, device_id_type=MESH
        )

    def weight_copy(target, slot):
        return remote(piece(half, target), mixes.at[half, slot], weight_send.at[target], weight_recv.at[slot], (target, group))

    def pass_copy(p, slot):
        return remote(mixes.at[p, slot], mixes.at[p, slot], pass_send.at[slot], pass_recv.at[slot], sibling)

    @pl.loop(1, chans)
    def _(k):
        weight_copy(lax.rem(chan + k, chans), chan).start()

    for copy in mine:
        copy.start()
    load.start()
    for copy in mine:
        copy.wait()

    def far_of(i):
        return lax.rem(far + i + 1, fars)

    def pass_on(slot):
        @pl.when(slot != chan)
        def _():
            weight_copy(slot, slot).wait_recv()
            pass_copy(half, slot).start()

    @pl.loop(0, fars)
    def _(i):
        pass_on(2 * far_of(i) + 1 - side)

    load.wait()

    def partial(slot):
        @pl.when(slot != chan)
        def _():
            pass_copy(1 - half, slot).wait_recv()

        channel = map_ref[slot]
        reals, imags = [], []
        for p in range(pols):
            mixed = jnp.concatenate([mixes[p, slot, 0], mixes[p, slot, 1]], axis=0)
            left = dot(mixed, volts[0, p, channel])
            right = dot(mixed, volts[1, p, channel])
            reals.append(left[:beams] - right[beams:])
            imags.append(left[beams:] + right[:beams])
        share = beams // groups
        return [
            jnp.concatenate([part[g * share : (g + 1) * share] for part in reals + imags], axis=0)
            for g in range(groups)
        ]

    def near_copies(i):
        return [
            remote(away_code.at[i], near_code.at[i], near_send.at[0, i], near_recv.at[0, i], partner),
            remote(away_step.at[i], near_step.at[i], near_send.at[1, i], near_recv.at[1, i], partner),
        ]

    @pl.loop(0, fars)
    def _(i):
        there = far_of(i)
        pass_on(2 * there + side)
        for g, rows in enumerate(partial(2 * there + 1 - side)):
            away_code[i, g], away_step[i, g] = encode(rows)
        for copy in near_copies(i):
            copy.start()

    def sum_copies(i, g, target, source):
        device = (2 * target + side, g)
        return [
            remote(sum_code.at[i, g], code_out.at[source], sum_send.at[0, i * groups + g], sum_recv.at[0, source], device),
            remote(sum_step.at[i, g], step_out.at[source], sum_send.at[1, i * groups + g], sum_recv.at[1, source], device),
        ]

    origin = far * groups + group

    @pl.loop(0, fars)
    def _(i):
        there = far_of(i)
        parts = partial(2 * there + side)
        for copy in near_copies(i):
            copy.wait_recv()
        for g, rows in enumerate(parts):
            sum_code[i, g], sum_step[i, g] = encode(rows + decode(near_code[i, g], near_step[i, g]))

            @pl.when((there != far) | (g != group))
            def _(g=g):
                for copy in sum_copies(i, g, there, origin):
                    copy.start()

    last = fars - 1
    kept = [
        pltpu.make_async_copy(sum_code.at[last, group], code_out.at[origin], own.at[0]),
        pltpu.make_async_copy(sum_step.at[last, group], step_out.at[origin], own.at[1]),
    ]
    for copy in kept:
        copy.start()

    @pl.loop(0, chans)
    def _(slot):
        @pl.when(slot != chan)
        def _():
            weight_copy(slot, slot).wait_send()
            pass_copy(half, slot).wait_send()

    @pl.loop(0, fars)
    def _(i):
        for copy in near_copies(i):
            copy.wait_send()
        there = far_of(i)
        for g in range(groups):
            @pl.when((there != far) | (g != group))
            def _(g=g):
                for copy in sum_copies(i, g, there, there * groups + g):
                    copy.wait_send()
                    copy.wait_recv()

    for copy in kept:
        copy.wait()


def form_sums(voltages, weights, channel_map, chans, groups):
    parts, pols, channels, antennas, times = voltages.shape
    beams = weights.shape[2]
    sliced = antennas % 128 == 0
    if not sliced:
        weights = weights.reshape(2, pols, beams, chans, antennas).transpose(3, 0, 1, 2, 4)
    rows = 2 * pols * beams // groups
    fars = chans // 2
    any_spec = pl.BlockSpec(memory_space=pl.ANY)
    code, step = (fars, groups, rows, times), (fars, groups, 1, times)
    dma = pltpu.SemaphoreType.DMA
    return pl.pallas_call(
        functools.partial(form_kernel, chans, groups, sliced),
        in_specs=[pl.BlockSpec(memory_space=pltpu.SMEM), any_spec, any_spec],
        out_specs=[any_spec, any_spec],
        out_shape=[
            jax.ShapeDtypeStruct((fars * groups, rows, times), jnp.int16),
            jax.ShapeDtypeStruct((fars * groups, 1, times), jnp.float32),
        ],
        scratch_shapes=[
            pltpu.VMEM(voltages.shape, voltages.dtype),
            pltpu.VMEM((pols, chans, 2, beams, antennas), weights.dtype),
        ]
        + [pltpu.VMEM(code, jnp.int16), pltpu.VMEM(step, jnp.float32)] * 3
        + [
            dma((pols + 1,)), dma((chans,)), dma((chans,)), dma((chans,)), dma((chans,)),
            dma((2, fars)), dma((2, fars)), dma((2, fars * groups)), dma((2, fars * groups)),
        ],
        compiler_params=pltpu.CompilerParams(collective_id=0, has_side_effects=True, vmem_limit_bytes=48 << 20),
        name="form_sums",
    )(channel_map, voltages, weights)


def split(value):
    high = value.astype(jnp.bfloat16)
    return high, (value - high.astype(jnp.float32)).astype(jnp.bfloat16)


def transform(value, high, low):
    rows = value.shape[0]
    first, second = split(value)
    both = dot(jnp.concatenate([first, second], axis=0), high)
    return both[:rows] + both[rows:] + dot(first, low)


def dedisperse_kernel(chans, groups, code_ref, step_ref, resp_ref, table_ref, out_ref, sums):
    longest, beams = resp_ref.shape[2], resp_ref.shape[1]
    rows, times = code_ref.shape[1], code_ref.shape[2]
    half = rows // 2
    for g in range(groups):

        def add(c, total, g=g):
            at = c * groups + g
            return total + decode(code_ref[at], step_ref[at])

        sums[g] = lax.fori_loop(0, chans, add, jnp.zeros((rows, times), jnp.float32))
    cos_high, cos_low, sin_high, sin_low = (table_ref[n] for n in range(4))
    resp = jnp.concatenate([resp_ref[0], resp_ref[1]], axis=0)
    by_cos = transform(resp, cos_high[:longest], cos_low[:longest])
    by_sin = transform(resp, sin_high[:longest], sin_low[:longest])
    gain_real = (by_cos[:beams] + by_sin[beams:])[None]
    gain_imag = (by_cos[beams:] - by_sin[:beams])[None]

    per = times // longest
    count = groups * per
    blocks = []
    for r in range(2):
        pieces = [jnp.zeros((half, longest), jnp.float32)]
        for m in range(count):
            pieces.append(sums[m // per, r * half : (r + 1) * half, (m % per) * longest : (m % per + 1) * longest])
        blocks += [jnp.concatenate([pieces[m], pieces[m + 1]], axis=1) for m in range(count)]
    stacked = jnp.concatenate(blocks, axis=0)
    size = count * half
    by_cos = transform(stacked, cos_high, cos_low)
    by_sin = transform(stacked, sin_high, sin_low)
    shape = (size // beams, beams, 2 * longest)
    spec_real = (by_cos[:size] + by_sin[size:]).reshape(shape)
    spec_imag = (by_cos[size:] - by_sin[:size]).reshape(shape)
    prod_real = (spec_real * gain_real - spec_imag * gain_imag).reshape(size, 2 * longest)
    prod_imag = (spec_real * gain_imag + spec_imag * gain_real).reshape(size, 2 * longest)
    stacked = jnp.concatenate([prod_real, prod_imag], axis=0) * (0.5 / longest)
    by_cos = transform(stacked, cos_high[:, longest:], cos_low[:, longest:])
    by_sin = transform(stacked, sin_high[:, longest:], sin_low[:, longest:])
    results = (by_cos[:size] - by_sin[size:], by_cos[size:] + by_sin[:size])
    for r in range(2):
        for m in range(count):
            for p in range(half // beams):
                start = m * half + p * beams
                out_ref[0, r, p, :, m * longest : (m + 1) * longest] = results[r][start : start + beams]


def dedisperse(codes, steps, resp, chans, groups):
    rows, times = codes.shape[1:]
    beams, longest = resp.shape[1:]
    return pl.pallas_call(
        functools.partial(dedisperse_kernel, chans, groups),
        in_specs=[pl.BlockSpec(memory_space=pltpu.VMEM)] * 4,
        out_specs=pl.BlockSpec(memory_space=pltpu.VMEM),
        out_shape=jax.ShapeDtypeStruct((1, 2, rows // (2 * beams), beams, groups * times), jnp.float32),
        scratch_shapes=[pltpu.VMEM((groups, rows, times), jnp.float32)],
        compiler_params=pltpu.CompilerParams(vmem_limit_bytes=40 << 20),
        name="dedisperse",
    )(codes, steps, resp, jnp.asarray(fourier_tables(2 * longest)))


def on_device(chans, groups, voltages, weights, channel_map, sweep_response_taps, chirp_length):
    longest = sweep_response_taps.shape[3]
    lag = jnp.arange(longest, dtype=jnp.int32)
    inside = lag[None, :] < chirp_length[:, None]
    factor = lax.rsqrt(chirp_length.astype(jnp.float32))[:, None]
    resp = jnp.where(inside, sweep_response_taps[0], 0.0) * factor
    codes, steps = form_sums(voltages, weights[0], channel_map, chans, groups)
    return dedisperse(codes, steps, resp, chans // 2, groups)


def solution(mesh):
    return jax.shard_map(
        functools.partial(on_device, mesh.shape["chan"], mesh.shape["tm"]),
        mesh=mesh,
        in_specs=(
            P(None, None, None, "chan", "tm"),
            P("chan", None, None, None, None),
            P(),
            P("chan", None, "tm", None),
            P("tm"),
        ),
        out_specs=P("chan", None, None, "tm", None),
        check_vma=False,
    )
```

time: 69.7 us -> 42.6 us (0.61)
  the two profiles are of different devices: /device:TPU:11 before, /device:TPU:5 now
where the time goes in v2:
time: 42.6 us; the launch traced here: 42 us
  Pallas kernels  38 us (89%)
  other arithmetic  2.33 us (5%)
  local copies, waits for them, and re-layouts  1.7 us (4%)
    pallas_call x1, Pallas kernels, form_sums(): pl.pallas_call(functools.partial(form_kernel, chans, groups, sliced), in_...  34.8 us
    pallas_call x1, Pallas kernels, dedisperse(): pl.pallas_call(functools.partial(dedisperse_kernel, chans, groups), in_sp...  3.23 us
    unnamed x6, local copies, waits for them, and re-layouts  1.7 us

profile of v2, /device:TPU:5, one launch (start us, length us, event | category | flops | bytes accessed | tf_op | source)
XLA Modules:
  0.0 42.0 jit_solution(14763097126251716641)
XLA Ops:
  0.0 0.0 copy-start
  0.0 0.8 %convert_rsqrt_fusion = f32[8]{0:T(128)S(1)} fusion(s32[8]{0:T(128)} %param.10), kind=kLoop, calls=%fused_computation.3 | loop fusion | flops 8 | bytes 64 | tf_op jit(solution)/shard_map/rsqrt | solution.py:306
  0.8 0.7 %iota_compare_fusion = pred[8,256]{1,0:T(8,128)(4,1)S(1)} fusion(s32[8]{0:T(128)} %param.10), kind=kLoop, calls=%fused_computation.2 | loop fusion | flops 2048 | bytes 2080 | tf_op jit(solution)/shard_map/lt | solution.py:305
  1.5 0.8 %fusion.resp_ref = f32[2,8,256]{2,1,0:T(8,128)S(1)} fusion(f32[1,2,8,256]{3,2,1,0:T(8,128)} %param.9, f32[8]{0:T(128)S(1)} %convert_rsqrt_fusion, pred[8,256]{1,0:T(8,128)(4,1)S(1)} %iota_compare_fusion), kind=kLoop, calls=%fused_computation.1 | loop fusion | flops 8192 | bytes 34848 | tf_op jit(solution)/shard_map/mul | solution.py:307
  2.3 0.0 copy-start.1
  2.3 1.0 %copy-done.1 = bf16[1,2,2,32,2048]{4,3,2,1,0:T(8,128)(2,1)S(1)} copy-done((bf16[1,2,2,32,2048]{4,3,2,1,0:T(8,128)(2,1)S(1)}, bf16[1,2,2,32,2048]{4,3,2,1,0:T(8,128)(2,1)}, u32[]{:S(2)}) %copy-start.1) | copy-done | bytes 524312
  3.4 0.0 copy-start.2
  3.4 0.7 %copy-done.2 = s32[8]{0:T(128)S(1)} copy-done((s32[8]{0:T(128)S(1)}, s32[8]{0:T(128)}, u32[]{:S(2)}) %copy-start.2) | copy-done | bytes 56
  4.0 34.8 %form_sums.1 = (s16[16,32,512]{2,1,0:T(8,128)(2,1)S(1)}, f32[16,1,512]{2,1,0:T(1,128)S(1)}) custom-call(s32[8]{0:T(128)S(1)} %copy-done.2, bf16[2,2,8,256,512]{4,3,2,1,0:T(8,128)(2,1)} %volt_ref.1, bf16[2,2,32,2048]{3,2,1,0:T(8,128)(2,1)S(1)} %bitcast.5), custom_call_target="tpu_custom_call" | custom-call | tf_op jit(solution)/shard_map/form_sums/pallas_call | solution.py:208
  38.8 0.0 copy-done
  38.8 3.2 %dedisperse.1 = f32[1,2,2,8,2048]{4,3,2,1,0:T(8,128)} custom-call(s16[16,32,512]{2,1,0:T(8,128)(2,1)S(1)} %get-tuple-element.7.code_ref, f32[16,1,512]{2,1,0:T(1,128)S(1)} %get-tuple-element.8.step_ref, f32[2,8,256]{2,1,0:T(8,128)S(1)} %fusion.resp_ref, bf16[4,512,512]{2,1,0:T(8,128)(2,1)S(1)} %copy-done), custom_call_target="tpu_custom_call" | custom-call | tf_op jit(solution)/shard_map/dedisperse/pallas_call | solution.py:291
Async XLA Ops:
  0.0 38.8 %copy-start = (bf16[4,512,512]{2,1,0:T(8,128)(2,1)S(1)}, bf16[4,512,512]{2,1,0:T(8,128)(2,1)}, u32[]{:S(2)}) copy-start(bf16[4,512,512]{2,1,0:T(8,128)(2,1)} %constant.4.clone.table_ref) | copy-start | bytes 6291460
  2.3 1.0 %copy-start.1 = (bf16[1,2,2,32,2048]{4,3,2,1,0:T(8,128)(2,1)S(1)}, bf16[1,2,2,32,2048]{4,3,2,1,0:T(8,128)(2,1)}, u32[]{:S(2)}) copy-start(bf16[1,2,2,32,2048]{4,3,2,1,0:T(8,128)(2,1)} %param.7) | copy-start | bytes 1572868
  3.4 0.7 %copy-start.2 = (s32[8]{0:T(128)S(1)}, s32[8]{0:T(128)}, u32[]{:S(2)}) copy-start(s32[8]{0:T(128)} %map_ref.1) | copy-start | bytes 100

commit v3 on v2

v3 whole, which is shorter than its diff:
```python
import functools
import math

import jax
import jax.numpy as jnp
import ml_dtypes
import numpy as np
from jax import lax
from jax.experimental import pallas as pl
from jax.experimental.pallas import tpu as pltpu
from jax.sharding import PartitionSpec as P

TOP = 32767.0
MESH = pl.DeviceIdType.MESH


def dot(left, right):
    return jnp.dot(left, right, preferred_element_type=jnp.float32)


def fourier_tables(extent):
    counter = np.arange(extent, dtype=np.int64)
    angle = (counter[:, None] * counter[None, :] % extent) * (2.0 * math.pi / extent)
    tables = []
    for table in (np.cos(angle), np.sin(angle)):
        high = table.astype(ml_dtypes.bfloat16)
        low = (table - high.astype(np.float64)).astype(ml_dtypes.bfloat16)
        tables += [high, low]
    return np.stack(tables)


def encode(rows):
    peak = jnp.maximum(jnp.max(jnp.abs(rows), axis=0, keepdims=True), 1e-30)
    codes = jnp.round(rows * (TOP / peak)).astype(jnp.int32).astype(jnp.int16)
    return codes, peak * (1.0 / TOP)


def decode(codes, step):
    return codes.astype(jnp.int32).astype(jnp.float32) * step


def split(value):
    high = value.astype(jnp.bfloat16)
    return high, (value - high.astype(jnp.float32)).astype(jnp.bfloat16)


def transform(value, high, low):
    rows = value.shape[0]
    first, second = split(value)
    both = dot(jnp.concatenate([first, second], axis=0), high)
    return both[:rows] + both[rows:] + dot(first, low)


def gains(chirp_ref, taps_ref, table_ref):
    beams, longest = taps_ref.shape[2], taps_ref.shape[3]
    row = lax.broadcasted_iota(jnp.int32, (beams, longest), 0)
    lag = lax.broadcasted_iota(jnp.int32, (beams, longest), 1)
    length = jnp.zeros((beams, longest), jnp.int32)
    for b in range(beams):
        length = jnp.where(row == b, chirp_ref[b], length)
    factor = 1.0 / jnp.sqrt(length.astype(jnp.float32))
    resp = jnp.concatenate([jnp.where(lag < length, taps_ref[0, r], 0.0) * factor for r in range(2)], axis=0)
    by_cos = transform(resp, table_ref[0, :longest], table_ref[1, :longest])
    by_sin = transform(resp, table_ref[2, :longest], table_ref[3, :longest])
    return by_cos[:beams] + by_sin[beams:], by_cos[beams:] - by_sin[:beams]


def dedisperse(sums, gain_real, gain_imag, table_ref, out_ref):
    groups, rows, times = sums.shape
    beams, longest = gain_real.shape[1], gain_real.shape[2] // 2
    half = rows // 2
    cos_high, cos_low, sin_high, sin_low = (table_ref[n] for n in range(4))
    per = times // longest
    count = groups * per
    blocks = []
    for r in range(2):
        pieces = [jnp.zeros((half, longest), jnp.float32)]
        for m in range(count):
            pieces.append(sums[m // per, r * half : (r + 1) * half, (m % per) * longest : (m % per + 1) * longest])
        blocks += [jnp.concatenate([pieces[m], pieces[m + 1]], axis=1) for m in range(count)]
    stacked = jnp.concatenate(blocks, axis=0)
    size = count * half
    by_cos = transform(stacked, cos_high, cos_low)
    by_sin = transform(stacked, sin_high, sin_low)
    shape = (size // beams, beams, 2 * longest)
    spec_real = (by_cos[:size] + by_sin[size:]).reshape(shape)
    spec_imag = (by_cos[size:] - by_sin[:size]).reshape(shape)
    prod_real = (spec_real * gain_real - spec_imag * gain_imag).reshape(size, 2 * longest)
    prod_imag = (spec_real * gain_imag + spec_imag * gain_real).reshape(size, 2 * longest)
    stacked = jnp.concatenate([prod_real, prod_imag], axis=0) * (0.5 / longest)
    by_cos = transform(stacked, cos_high[:, longest:], cos_low[:, longest:])
    by_sin = transform(stacked, sin_high[:, longest:], sin_low[:, longest:])
    results = (by_cos[:size] - by_sin[size:], by_cos[size:] + by_sin[:size])
    for r in range(2):
        for m in range(count):
            for p in range(half // beams):
                start = m * half + p * beams
                out_ref[0, r, p, :, m * longest : (m + 1) * longest] = results[r][start : start + beams]


def form_kernel(
    chans, groups, sliced, map_ref, chirp_ref, volt_ref, weight_ref, table_hbm, taps_ref, out_ref,
    volts, mixes, tables, code_out, step_out, gain, sums, away_code, away_step, near_code, near_step, sum_code, sum_step,
    own, weight_send, weight_recv, pass_send, pass_recv, near_send, near_recv, sum_send, sum_recv,
):
    pols, beams, antennas = mixes.shape[0], mixes.shape[3], mixes.shape[4]
    chan, group = lax.axis_index("chan"), lax.axis_index("tm")
    far, side = lax.div(chan, 2), lax.rem(chan, 2)
    fars = chans // 2
    half = lax.rem(group, 2)
    sibling = (chan, group + 1 - 2 * half)
    partner = (chan + 1 - 2 * side, group)
    total = chans * groups
    me = chan * groups + group
    barrier = pltpu.get_barrier_semaphore()
    table_load = pltpu.make_async_copy(table_hbm, tables, own.at[pols + 1])
    table_load.start()
    load = pltpu.make_async_copy(volt_ref, volts, own.at[pols])
    load.start()

    @pl.loop(1, total)
    def _(k):
        other = lax.rem(me + k, total)
        device = (lax.div(other, groups), lax.rem(other, groups))
        pl.semaphore_signal(barrier, inc=1, device_id=device, device_id_type=MESH)

    def piece(p, target):
        if sliced:
            return weight_ref.at[:, p, :, pl.ds(pl.multiple_of(target * antennas, antennas), antennas)]
        return weight_ref.at[target, :, p]

    mine = [pltpu.make_async_copy(piece(p, chan), mixes.at[p, chan], own.at[p]) for p in range(pols)]
    for copy in mine:
        copy.start()
    pl.semaphore_wait(barrier, total - 1)

    def remote(source, target, send, recv, device):
        return pltpu.make_async_remote_copy(
            src_ref=source, dst_ref=target, send_sem=send, recv_sem=recv, device_id=device, device_id_type=MESH
        )

    def weight_copy(target, slot):
        return remote(piece(half, target), mixes.at[half, slot], weight_send.at[target], weight_recv.at[slot], (target, group))

    def pass_copy(p, slot):
        return remote(mixes.at[p, slot], mixes.at[p, slot], pass_send.at[slot], pass_recv.at[slot], sibling)

    @pl.loop(0, fars)
    def _(i):
        weight_copy(2 * lax.rem(far + fars - 1 - i, fars) + 1 - side, chan).start()

    @pl.loop(0, fars - 1)
    def _(i):
        weight_copy(2 * lax.rem(far + fars - 1 - i, fars) + side, chan).start()

    table_load.wait()
    gain[0], gain[1] = gains(chirp_ref, taps_ref, tables)
    for copy in mine:
        copy.wait()

    def far_of(i):
        return lax.rem(far + i + 1, fars)

    def pass_on(slot):
        @pl.when(slot != chan)
        def _():
            weight_copy(slot, slot).wait_recv()
            pass_copy(half, slot).start()

    def turn(i):
        there = far_of(lax.rem(i, fars))
        return 2 * there + jnp.where(i < fars, 1 - side, side)

    pass_on(turn(0))
    load.wait()

    def partial(slot):
        @pl.when(slot != chan)
        def _():
            pass_copy(1 - half, slot).wait_recv()

        channel = map_ref[slot]
        reals, imags = [], []
        for p in range(pols):
            mixed = jnp.concatenate([mixes[p, slot, 0], mixes[p, slot, 1]], axis=0)
            left = dot(mixed, volts[0, p, channel])
            right = dot(mixed, volts[1, p, channel])
            reals.append(left[:beams] - right[beams:])
            imags.append(left[beams:] + right[:beams])
        share = beams // groups
        return [
            jnp.concatenate([part[g * share : (g + 1) * share] for part in reals + imags], axis=0)
            for g in range(groups)
        ]

    def near_copies(i):
        return [
            remote(away_code.at[i], near_code.at[i], near_send.at[0, i], near_recv.at[0, i], partner),
            remote(away_step.at[i], near_step.at[i], near_send.at[1, i], near_recv.at[1, i], partner),
        ]

    @pl.loop(0, fars)
    def _(i):
        there = far_of(i)
        pass_on(turn(i + 1))
        for g, rows in enumerate(partial(2 * there + 1 - side)):
            away_code[i, g], away_step[i, g] = encode(rows)
        for copy in near_copies(i):
            copy.start()

    def sum_copies(i, g, target, source):
        device = (2 * target + side, g)
        return [
            remote(sum_code.at[i, g], code_out.at[source], sum_send.at[0, i * groups + g], sum_recv.at[0, source], device),
            remote(sum_step.at[i, g], step_out.at[source], sum_send.at[1, i * groups + g], sum_recv.at[1, source], device),
        ]

    origin = far * groups + group

    @pl.loop(0, fars)
    def _(i):
        there = far_of(i)

        @pl.when(i < fars - 1)
        def _():
            pass_on(turn(fars + i + 1))

        parts = partial(2 * there + side)
        for copy in near_copies(i):
            copy.wait_recv()
        for g, rows in enumerate(parts):
            sum_code[i, g], sum_step[i, g] = encode(rows + decode(near_code[i, g], near_step[i, g]))

            @pl.when((there != far) | (g != group))
            def _(g=g):
                for copy in sum_copies(i, g, there, origin):
                    copy.start()

    last = fars - 1
    kept = [
        pltpu.make_async_copy(sum_code.at[last, group], code_out.at[origin], own.at[0]),
        pltpu.make_async_copy(sum_step.at[last, group], step_out.at[origin], own.at[1]),
    ]
    for copy in kept:
        copy.start()

    for copy in kept:
        copy.wait()
    sums[...] = jnp.zeros(sums.shape, sums.dtype)

    @pl.loop(0, fars)
    def _(i):
        there = lax.rem(far + fars - 1 - i, fars)
        for g in range(groups):
            at = there * groups + g

            @pl.when((there != far) | (g != group))
            def _(at=at, g=g):
                for copy in sum_copies(0, g, there, at):
                    copy.wait_recv()

            sums[g] += decode(code_out[at], step_out[at])

    dedisperse(sums, gain[0:1], gain[1:2], tables, out_ref)

    @pl.loop(0, chans)
    def _(slot):
        @pl.when(slot != chan)
        def _():
            weight_copy(slot, slot).wait_send()
            pass_copy(half, slot).wait_send()

    @pl.loop(0, fars)
    def _(i):
        for copy in near_copies(i):
            copy.wait_send()
        there = far_of(i)
        for g in range(groups):
            @pl.when((there != far) | (g != group))
            def _(g=g):
                for copy in sum_copies(i, g, there, origin):
                    copy.wait_send()


def form_series(voltages, weights, channel_map, taps, chirp_length, chans, groups):
    parts, pols, channels, antennas, times = voltages.shape
    beams = weights.shape[2]
    sliced = antennas % 128 == 0
    if not sliced:
        weights = weights.reshape(2, pols, beams, chans, antennas).transpose(3, 0, 1, 2, 4)
    rows, share, longest = 2 * pols * beams // groups, beams // groups, taps.shape[3]
    fars = chans // 2
    table = jnp.asarray(fourier_tables(2 * longest))
    any_spec = pl.BlockSpec(memory_space=pl.ANY)
    code, step = (fars, groups, rows, times), (fars, groups, 1, times)
    dma = pltpu.SemaphoreType.DMA
    return pl.pallas_call(
        functools.partial(form_kernel, chans, groups, sliced),
        in_specs=[pl.BlockSpec(memory_space=pltpu.SMEM)] * 2 + [any_spec] * 3 + [pl.BlockSpec(memory_space=pltpu.VMEM)],
        out_specs=pl.BlockSpec(memory_space=pltpu.VMEM),
        out_shape=jax.ShapeDtypeStruct((1, 2, pols, share, groups * times), jnp.float32),
        scratch_shapes=[
            pltpu.VMEM(voltages.shape, voltages.dtype),
            pltpu.VMEM((pols, chans, 2, beams, antennas), weights.dtype),
            pltpu.VMEM(table.shape, table.dtype),
            pltpu.VMEM((fars * groups, rows, times), jnp.int16),
            pltpu.VMEM((fars * groups, 1, times), jnp.float32),
            pltpu.VMEM((2, share, 2 * longest), jnp.float32),
            pltpu.VMEM((groups, rows, times), jnp.float32),
        ]
        + [pltpu.VMEM(code, jnp.int16), pltpu.VMEM(step, jnp.float32)] * 3
        + [
            dma((pols + 2,)), dma((chans,)), dma((chans,)), dma((chans,)), dma((chans,)),
            dma((2, fars)), dma((2, fars)), dma((2, fars * groups)), dma((2, fars * groups)),
        ],
        compiler_params=pltpu.CompilerParams(collective_id=0, has_side_effects=True, vmem_limit_bytes=56 << 20),
        name="form_series",
    )(channel_map, chirp_length, voltages, weights, table, taps)


def on_device(chans, groups, voltages, weights, channel_map, sweep_response_taps, chirp_length):
    return form_series(voltages, weights[0], channel_map, sweep_response_taps, chirp_length, chans, groups)


def solution(mesh):
    return jax.shard_map(
        functools.partial(on_device, mesh.shape["chan"], mesh.shape["tm"]),
        mesh=mesh,
        in_specs=(
            P(None, None, None, "chan", "tm"),
            P("chan", None, None, None, None),
            P(),
            P("chan", None, "tm", None),
            P("tm"),
        ),
        out_specs=P("chan", None, None, "tm", None),
        check_vma=False,
    )
```

time: 42.6 us -> 37.6 us (0.88)
  other arithmetic: 2.33 us -> 0 us
  Pallas kernels: 38 us -> 35.7 us
    pallas_call x2 -> x1, Pallas kernels: 38 us -> 35.7 us  [form_series(): pl.pallas_call(functools.partial(form_kernel, chans, groups, sliced), in_...]
    rsqrt x1 -> x0, other arithmetic: 0.81 us -> none  [on_device(): factor = lax.rsqrt(chirp_length.astype(jnp.float32))[:, None]]
    mul x1 -> x0, other arithmetic: 0.79 us -> none  [on_device(): resp = jnp.where(inside, sweep_response_taps[0], 0.0) * factor]
    lt x1 -> x0, other arithmetic: 0.73 us -> none  [on_device(): inside = lag[None, :] < chirp_length[:, None]]
    unnamed x6 -> x1, local copies, waits for them, and re-layouts: 1.7 us -> 1.67 us
where the time goes in v3:
time: 37.6 us; the launch traced here: 37.3 us
  Pallas kernels  35.7 us (95%)
  local copies, waits for them, and re-layouts  1.67 us (4%)
    pallas_call x1, Pallas kernels, form_series(): pl.pallas_call(functools.partial(form_kernel, chans, groups, sliced), in_...  35.7 us
    unnamed x1, local copies, waits for them, and re-layouts  1.67 us

profile of v3, /device:TPU:5, one launch (start us, length us, event | category | flops | bytes accessed | tf_op | source)
XLA Modules:
  0.0 37.3 jit_solution(15119687482916506657)
XLA Ops:
  0.0 35.7 %form_series.1 = f32[1,2,2,8,2048]{4,3,2,1,0:T(8,128)} custom-call(s32[8]{0:T(128)} %map_ref.1, s32[8]{0:T(128)} %chirp_ref.1, bf16[2,2,8,256,512]{4,3,2,1,0:T(8,128)(2,1)} %volt_ref.1, bf16[2,2,32,2048]{3,2,1,0:T(8,128)(2,1)} %bitcast.1, bf16[4,512,512]{2,1,0:T(8,128)(2,1)} %constant.2.clone.table_hbm, f32[1,2,8,256]{3,2,1,0:T(8,128)} %taps_ref.1), custom_call_target="tpu_custom_call" | custom-call | tf_op jit(solution)/shard_map/form_series/pallas_call | solution.py:297
  35.7 1.7 %copy.8 = f32[1,2,2,8,2048]{4,3,2,1,0:T(8,128)} copy(f32[1,2,2,8,2048]{4,3,2,1,0:T(8,128)} %form_series.1) | data formatting | bytes 524288

commit v4 on v3

--- a/solution.py
+++ b/solution.py
@@ -29,8 +29,11 @@
     return np.stack(tables)
 
 
-def encode(rows):
-    peak = jnp.maximum(jnp.max(jnp.abs(rows), axis=0, keepdims=True), 1e-30)
+def peak_of(rows):
+    return jnp.maximum(jnp.max(jnp.abs(rows), axis=0, keepdims=True), 1e-30)
+
+
+def encode(rows, peak):
     codes = jnp.round(rows * (TOP / peak)).astype(jnp.int32).astype(jnp.int16)
     return codes, peak * (1.0 / TOP)
 
@@ -110,19 +113,21 @@
     half = lax.rem(group, 2)
     sibling = (chan, group + 1 - 2 * half)
     partner = (chan + 1 - 2 * side, group)
-    total = chans * groups
-    me = chan * groups + group
     barrier = pltpu.get_barrier_semaphore()
     table_load = pltpu.make_async_copy(table_hbm, tables, own.at[pols + 1])
     table_load.start()
     load = pltpu.make_async_copy(volt_ref, volts, own.at[pols])
     load.start()
 
-    @pl.loop(1, total)
+    @pl.loop(1, chans)
     def _(k):
-        other = lax.rem(me + k, total)
-        device = (lax.div(other, groups), lax.rem(other, groups))
-        pl.semaphore_signal(barrier, inc=1, device_id=device, device_id_type=MESH)
+        pl.semaphore_signal(barrier, inc=1, device_id=(lax.rem(chan + k, chans), group), device_id_type=MESH)
+
+    @pl.loop(0, fars)
+    def _(k):
+        for d in range(1, groups):
+            device = (2 * lax.rem(far + k, fars) + side, lax.rem(group + d, groups))
+            pl.semaphore_signal(barrier, inc=1, device_id=device, device_id_type=MESH)
 
     def piece(p, target):
         if sliced:
@@ -132,7 +137,9 @@
     mine = [pltpu.make_async_copy(piece(p, chan), mixes.at[p, chan], own.at[p]) for p in range(pols)]
     for copy in mine:
         copy.start()
-    pl.semaphore_wait(barrier, total - 1)
+    table_load.wait()
+    gain[0], gain[1] = gains(chirp_ref, taps_ref, tables)
+    pl.semaphore_wait(barrier, chans - 1 + fars * (groups - 1))
 
     def remote(source, target, send, recv, device):
         return pltpu.make_async_remote_copy(
@@ -153,8 +160,6 @@
     def _(i):
         weight_copy(2 * lax.rem(far + fars - 1 - i, fars) + side, chan).start()
 
-    table_load.wait()
-    gain[0], gain[1] = gains(chirp_ref, taps_ref, tables)
     for copy in mine:
         copy.wait()
 
@@ -203,8 +208,10 @@
     def _(i):
         there = far_of(i)
         pass_on(turn(i + 1))
-        for g, rows in enumerate(partial(2 * there + 1 - side)):
-            away_code[i, g], away_step[i, g] = encode(rows)
+        parts = partial(2 * there + 1 - side)
+        peak = functools.reduce(jnp.maximum, [peak_of(rows) for rows in parts])
+        for g, rows in enumerate(parts):
+            away_code[i, g], away_step[i] = encode(rows, peak)
         for copy in near_copies(i):
             copy.start()
 
@@ -229,7 +236,8 @@
         for copy in near_copies(i):
             copy.wait_recv()
         for g, rows in enumerate(parts):
-            sum_code[i, g], sum_step[i, g] = encode(rows + decode(near_code[i, g], near_step[i, g]))
+            rows += decode(near_code[i, g], near_step[i])
+            sum_code[i, g], sum_step[i, g] = encode(rows, peak_of(rows))
 
             @pl.when((there != far) | (g != group))
             def _(g=g):
@@ -308,7 +316,8 @@
             pltpu.VMEM((2, share, 2 * longest), jnp.float32),
             pltpu.VMEM((groups, rows, times), jnp.float32),
         ]
-        + [pltpu.VMEM(code, jnp.int16), pltpu.VMEM(step, jnp.float32)] * 3
+        + [pltpu.VMEM(code, jnp.int16), pltpu.VMEM((fars, 1, times), jnp.float32)] * 2
+        + [pltpu.VMEM(code, jnp.int16), pltpu.VMEM(step, jnp.float32)]
         + [
             dma((pols + 2,)), dma((chans,)), dma((chans,)), dma((chans,)), dma((chans,)),
             dma((2, fars)), dma((2, fars)), dma((2, fars * groups)), dma((2, fars * groups)),

time: 37.6 us -> 36.3 us (0.965)
  Pallas kernels: 35.7 us -> 34.2 us
    pallas_call x1, Pallas kernels: 35.7 us -> 34.2 us  [form_series(): pl.pallas_call(functools.partial(form_kernel, chans, groups, sliced), in_...]
where the time goes in v4:
time: 36.3 us; the launch traced here: 35.8 us
  Pallas kernels  34.2 us (94%)
  local copies, waits for them, and re-layouts  1.67 us (5%)
    pallas_call x1, Pallas kernels, form_series(): pl.pallas_call(functools.partial(form_kernel, chans, groups, sliced), in_...  34.2 us
    unnamed x1, local copies, waits for them, and re-layouts  1.67 us

profile of v4, /device:TPU:5, one launch (start us, length us, event | category | flops | bytes accessed | tf_op | source)
XLA Modules:
  0.0 35.8 jit_solution(4946745134623681572)
XLA Ops:
  0.0 34.2 %form_series.1 = f32[1,2,2,8,2048]{4,3,2,1,0:T(8,128)} custom-call(s32[8]{0:T(128)} %map_ref.1, s32[8]{0:T(128)} %chirp_ref.1, bf16[2,2,8,256,512]{4,3,2,1,0:T(8,128)(2,1)} %volt_ref.1, bf16[2,2,32,2048]{3,2,1,0:T(8,128)(2,1)} %bitcast.1, bf16[4,512,512]{2,1,0:T(8,128)(2,1)} %constant.2.clone.table_hbm, f32[1,2,8,256]{3,2,1,0:T(8,128)} %taps_ref.1), custom_call_target="tpu_custom_call" | custom-call | tf_op jit(solution)/shard_map/form_series/pallas_call | solution.py:305
  34.2 1.7 %copy.8 = f32[1,2,2,8,2048]{4,3,2,1,0:T(8,128)} copy(f32[1,2,2,8,2048]{4,3,2,1,0:T(8,128)} %form_series.1) | data formatting | bytes 524288
